TPU v7x, 32 devices: a whole 2x2x4 slice. The times are simulated.
32 devices in a mesh: groups: 2 (over y), gx: 16 (over z, x, core).
Axes of the slice: x: 2, y: 2, z: 4, core: 2. Of those that a mesh axis runs over, the one named last changes fastest.
Arguments:
- attention: bfloat16 [1024, 16384], P('groups', 'gx'), parts along dimension 0, may hold values from -6 to 6
- activated: bfloat16 [1024, 26624], P('groups', 'gx'), parts along dimension 0, may hold values from -6 to 6
- residual: bfloat16 [1024, 16384], P('groups', 'gx'), parts along dimension 0, may hold values from -90 to 90
- out_tiles: bfloat16 [16, 2048, 8192], P('gx'), may hold values from -0.046875 to 0.046875
- down_tiles: bfloat16 [16, 3328, 8192], P('gx'), may hold values from -0.0390625 to 0.0390625
- norm_gain: bfloat16 [16384], P('gx'), may hold values from 0.5 to 1.5
Outputs:
- stream: bfloat16 [1024, 16384], P('groups', 'gx'), parts along dimension 0
- normed: bfloat16 [1024, 16384], P('groups', 'gx'), parts along dimension 0
There are 2 independent parts, one for each index of `groups`. A program takes and returns all parts, laid end to end along the dimension named above; an argument that names none is the same for every part. Nothing has to cross between parts.
All inputs are finite; a program needn't handle non-finite values.
Results may differ from a plain program's by a relative error of at most 0.0049.
Values may be sent and summed in bfloat16 or wider, within the bound.
A program may use at most 320 MiB of HBM per device.

v0:
```python
import jax
import jax.numpy as jnp
from jax import lax
from jax.sharding import PartitionSpec as P

D = 16384
COLB = 8


def shifted(block, axis, distance):
    devices = range(lax.axis_size(axis))
    route = [((i - distance) % len(devices), i) for i in devices]
    return lax.ppermute(block, axis, route)


def from_partner(array, axis, stride):
    return lax.ppermute(array, axis, [(i, i ^ 1 << stride) for i in range(lax.axis_size(axis))])


def forward_move(pieces):
    return shifted((pieces[0], pieces[1]), "gx", COLB)


def body(attention, activated, residual, out_tiles, down_tiles, norm_gain):
    tile_out = out_tiles[0]
    tile_down = down_tiles[0]
    tok_rows = attention.shape[0]
    width_a = attention.shape[1]
    width_h = activated.shape[1]
    block_cols = tile_out.shape[1]
    shards = lax.axis_size("gx")
    row_groups = shards // COLB
    place = lax.axis_index("gx")
    own_group = place // COLB

    def contribute(carry, pieces, group_index):
        rows_out = lax.dynamic_slice_in_dim(tile_out, group_index * width_a, width_a, 0)
        rows_down = lax.dynamic_slice_in_dim(tile_down, group_index * width_h, width_h, 0)
        carry = carry + jnp.dot(pieces[0], rows_out, preferred_element_type=jnp.float32)
        return carry + jnp.dot(pieces[1], rows_down, preferred_element_type=jnp.float32)

    initial = jnp.zeros((tok_rows, block_cols), jnp.float32)
    own_pieces = (attention, activated)

    def advance_one(step, state):
        total, pieces = state
        total = contribute(total, pieces, (own_group - step) % row_groups)
        return (total, forward_move(pieces))

    carry, pieces = lax.fori_loop(0, row_groups - 1, advance_one, (initial, own_pieces))
    carry = contribute(carry, pieces, (own_group - row_groups + 1) % row_groups)
    levels = COLB.bit_length() - 1
    partial_value = carry
    for bit in range(levels - 1, -1, -1):
        half = partial_value.shape[1] // 2
        lower = partial_value[:, :half]
        upper = partial_value[:, half:]
        upper_side = place >> bit & 1 == 1
        keep = jnp.where(upper_side, upper, lower)
        sent = jnp.where(upper_side, lower, upper)
        partial_value = keep + from_partner(sent, "gx", bit)
    total = partial_value
    total = total + residual.astype(jnp.float32)
    stream = total.astype(jnp.bfloat16)
    wide = stream.astype(jnp.float32)
    local_sq = jnp.sum(wide * wide, axis=1)
    summed = lax.psum(local_sq, "gx")
    mean_square = summed[:, None] / D
    normed = wide * lax.rsqrt(mean_square + 1e-05) * norm_gain.astype(jnp.float32)[None, :]
    return (stream, normed.astype(jnp.bfloat16))


def solution(mesh):
    placed = (
        P("groups", "gx"),
        P("groups", "gx"),
        P("groups", "gx"),
        P("gx", None, None),
        P("gx", None, None),
        P("gx"),
    )
    return jax.shard_map(
        body,
        mesh=mesh,
        in_specs=placed,
        out_specs=(P("groups", "gx"), P("groups", "gx")),
        check_vma=False,
    )
```

profile of v0, /device:TPU:0, one launch (start us, length us, event | category | flops | bytes accessed | tf_op | source)
XLA Modules:
  0.0 513.2 jit_solution(16352662069434711618)
XLA Ops:
  0.6 4.1 collective-permute-start
  4.7 0.1 collective-permute-start.1
  4.8 24.4 %fusion.2 = f32[8192,512]{1,0:T(8,128)} fusion(bf16[512,1664]{1,0:T(8,128)(2,1)} %param.7, bf16[1,3328,8192]{2,1,0:T(8,128)(2,1)} %param.10, s32[]{:T(128)S(6)} %select_n.73), kind=kOutput, calls=%fused_computation.2 | convolution fusion | flops 13958643712 | bytes 45744132 | tf_op jit(solution)/shard_map/while/body/eval_jaxpr/dot_general | solution.py:40
  29.2 0.0 copy-done.4
  29.2 15.8 %fusion.8 = f32[8192,512]{1,0:T(8,128)} fusion(bf16[512,1024]{1,0:T(8,128)(2,1)S(1)} %copy-done.4, bf16[1,2048,8192]{2,1,0:T(8,128)(2,1)} %param.9, s32[]{:T(128)S(6)} %select_n.72), kind=kOutput, calls=%fused_computation.8 | convolution fusion | flops 8589934592 | bytes 34603012 | tf_op jit(solution)/shard_map/while/body/eval_jaxpr/dot_general | solution.py:39
  45.0 43.0 %collective-permute-done = bf16[512,1024]{1,0:T(8,128)(2,1)} collective-permute-done((bf16[512,1024]{1,0:T(8,128)(2,1)}, bf16[512,1024]{1,0:T(8,128)(2,1)}, u32[]{:S(2)}, u32[]{:S(2)}) %collective-permute-start) | collective-permute-done | bytes 1048608 | tf_op jit(solution)/shard_map/while/body/eval_jaxpr/ppermute | solution.py:13
  88.0 16.0 %fusion.6 = f32[8192,512]{1,0:T(8,128)} fusion(bf16[512,1024]{1,0:T(8,128)(2,1)} %collective-permute-done, bf16[1,2048,8192]{2,1,0:T(8,128)(2,1)} %param.9, s32[]{:T(128)S(6)} %select_n.75), kind=kOutput, calls=%fused_computation.6 | convolution fusion | flops 8589934592 | bytes 34603012 | tf_op jit(solution)/shard_map/dot_general | solution.py:39
  104.0 19.6 %collective-permute-done.1 = bf16[512,1664]{1,0:T(8,128)(2,1)S(1)} collective-permute-done((bf16[512,1664]{1,0:T(8,128)(2,1)}, bf16[512,1664]{1,0:T(8,128)(2,1)S(1)}, u32[]{:S(2)}, u32[]{:S(2)}) %collective-permute-start.1) | collective-permute-done | bytes 1703968 | tf_op jit(solution)/shard_map/while/body/eval_jaxpr/ppermute | solution.py:13
  123.6 32.9 %add_bitcast_fusion = f32[512,8192]{0,1:T(8,128)} fusion(f32[8192,512]{1,0:T(8,128)} %fusion.6, f32[8192,512]{1,0:T(8,128)} %fusion.8, f32[8192,512]{1,0:T(8,128)} %fusion.2, bf16[512,1664]{1,0:T(8,128)(2,1)S(1)} %collective-permute-done.1, bf16[1,3328,8192]{2,1,0:T(8,128)(2,1)} %param.10, s32[]{:T(128)S(6)} %select_n.76), kind=kOutput, calls=%fused_computation.10 | convolution fusion | flops 13971226624 | bytes 96075776 | tf_op jit(solution)/shard_map/dot_general | solution.py:40
  156.5 11.1 %slice_select_fusion = f32[512,4096]{0,1:T(8,128)} fusion(f32[512,8192]{0,1:T(8,128)} %add_bitcast_fusion, pred[]{:T(512)S(6)} %eq.15), kind=kLoop, calls=%fused_computation.14 | loop fusion | flops 2097152 | bytes 25165824 | tf_op jit(solution)/shard_map/jit(_where)/select_n | solution.py:60
  167.6 0.8 collective-permute-start.2
  168.4 181.1 %collective-permute-done.2 = f32[512,4096]{0,1:T(8,128)} collective-permute-done((f32[512,4096]{0,1:T(8,128)}, f32[512,4096]{0,1:T(8,128)}, u32[]{:S(2)}, u32[]{:S(2)}) %collective-permute-start.2) | collective-permute-done | bytes 8388640 | tf_op jit(solution)/shard_map/ppermute | solution.py:17
  349.6 9.8 %select_add_fusion = f32[512,4096]{0,1:T(8,128)S(1)} fusion(f32[512,4096]{0,1:T(8,128)} %collective-permute-done.2, f32[512,8192]{0,1:T(8,128)} %add_bitcast_fusion, pred[]{:T(512)S(6)} %eq.15), kind=kLoop, calls=%fused_computation.13 | loop fusion | flops 4194304 | bytes 33554432 | tf_op jit(solution)/shard_map/add | solution.py:61
  359.4 0.0 copy-start
  359.4 3.2 copy-done
  362.6 3.0 slice_select_fusion.1
  365.6 1.3 collective-permute-start.3
  366.9 89.8 %collective-permute-done.3 = f32[512,2048]{0,1:T(8,128)} collective-permute-done((f32[512,2048]{0,1:T(8,128)}, f32[512,2048]{0,1:T(8,128)}, u32[]{:S(2)}, u32[]{:S(2)}) %collective-permute-start.3) | collective-permute-done | bytes 4194336 | tf_op jit(solution)/shard_map/ppermute | solution.py:17
  456.7 6.2 %select_add_fusion.1 = f32[512,2048]{0,1:T(8,128)S(1)} fusion(f32[512,2048]{0,1:T(8,128)} %collective-permute-done.3, f32[512,4096]{0,1:T(8,128)} %copy-done, pred[]{:T(512)S(6)} %eq.14), kind=kLoop, calls=%fused_computation.15 | loop fusion | flops 2097152 | bytes 16777216 | tf_op jit(solution)/shard_map/add | solution.py:61
  462.9 0.0 copy-start.1
  462.9 1.9 copy-done.1
  464.9 1.8 slice_select_fusion.2
  466.7 0.0 collective-permute-start.4
  466.7 0.0 copy-done.2
  466.7 0.5 copy.8
  467.2 0.0 copy-done.3
  467.3 3.9 collective-permute-done.4
  471.2 3.8 fusion.12
  474.9 35.3 %psum.7 = f32[512]{0:T(512)S(1)} all-reduce(f32[512]{0:T(512)S(1)} %get-tuple-element.20), channel_id=1, replica_groups=mesh['groups'=2,'gx'=16] {'gx'}, use_global_device_ids=true, to_apply=%region_1.2 | all-reduce | flops 512 | bytes 4096 | tf_op jit(solution)/shard_map/psum | solution.py:67
  510.3 1.3 copy.9
  511.6 0.3 fusion.14
  511.9 1.3 copy.10
  (5 shorter events, 0.0 us)
Async XLA Ops:
  0.6 87.4 %collective-permute-start = (bf16[512,1024]{1,0:T(8,128)(2,1)}, bf16[512,1024]{1,0:T(8,128)(2,1)}, u32[]{:S(2)}, u32[]{:S(2)}) collective-permute-start(bf16[512,1024]{1,0:T(8,128)(2,1)} %param.6), channel_id=1, source_target_pairs={{8,0},{9,1},{10,2},{11,3},{12,4},{13,5},{14,6},{15,7},{0,8},{1,9},... | collective-permute-start | bytes 3145736 | tf_op jit(solution)/shard_map/while/body/eval_jaxpr/ppermute | solution.py:13
  4.7 118.9 %collective-permute-start.1 = (bf16[512,1664]{1,0:T(8,128)(2,1)}, bf16[512,1664]{1,0:T(8,128)(2,1)S(1)}, u32[]{:S(2)}, u32[]{:S(2)}) collective-permute-start(bf16[512,1664]{1,0:T(8,128)(2,1)} %param.7), channel_id=1, source_target_pairs={{8,0},{9,1},{10,2},{11,3},{12,4},{13,5},{14,6},{15,7},{0,8},{1,9},... | collective-permute-start | bytes 5111816 | tf_op jit(solution)/shard_map/while/body/eval_jaxpr/ppermute | solution.py:13
  4.8 24.4 %copy-start.4 = (bf16[512,1024]{1,0:T(8,128)(2,1)S(1)}, bf16[512,1024]{1,0:T(8,128)(2,1)}, u32[]{:S(2)}) copy-start(bf16[512,1024]{1,0:T(8,128)(2,1)} %param.6) | copy-start | bytes 3145732
  167.6 181.9 %collective-permute-start.2 = (f32[512,4096]{0,1:T(8,128)}, f32[512,4096]{0,1:T(8,128)}, u32[]{:S(2)}, u32[]{:S(2)}) collective-permute-start(f32[512,4096]{0,1:T(8,128)} %slice_select_fusion), channel_id=1, source_target_pairs={{0,4},{1,5},{2,6},{3,7},{4,0},{5,1},{6,2},{7,3},{8,12},{9,13},{10,... | collective-permute-start | bytes 25165832 | tf_op jit(solution)/shard_map/ppermute | solution.py:17
  359.4 3.2 copy-start
  365.6 91.1 %collective-permute-start.3 = (f32[512,2048]{0,1:T(8,128)}, f32[512,2048]{0,1:T(8,128)}, u32[]{:S(2)}, u32[]{:S(2)}) collective-permute-start(f32[512,2048]{0,1:T(8,128)} %slice_select_fusion.1), channel_id=1, source_target_pairs={{0,2},{1,3},{2,0},{3,1},{4,6},{5,7},{6,4},{7,5},{8,10},{9,11},{10,... | collective-permute-start | bytes 12582920 | tf_op jit(solution)/shard_map/ppermute | solution.py:17
  366.9 99.8 %copy-start.2 = (bf16[512,1024]{1,0:T(8,128)(2,1)S(1)}, bf16[512,1024]{1,0:T(8,128)(2,1)}, u32[]{:S(2)}) copy-start(bf16[512,1024]{1,0:T(8,128)(2,1)} %param.8) | copy-start | bytes 3145732
  462.9 1.9 copy-start.1
  464.9 2.4 copy-start.3
  466.7 4.5 collective-permute-start.4
where the time goes:
time: 513 us
  waiting for transfers between devices  337 us (66%)
  matrix products  89.2 us (17%)
  other arithmetic  36 us (7%)
  blocking collectives  35.3 us (7%)
  local copies, waits for them, and re-layouts  8.32 us (2%)
  starting transfers between devices  6.34 us (1%)
    ppermute x3, waiting for transfers between devices, from_partner(): lax.ppermute(array, axis, [(i, i ^ 1 << stride) for i in range(lax.axis_s...  275 us
    ppermute x2, waiting for transfers between devices, shifted(): return lax.ppermute(block, axis, route)  62.5 us
    dot_general x2, matrix products, contribute(): jnp.dot(pieces[1], rows_down, preferred_element_type=jnp.float32)  57.3 us
    psum x1, blocking collectives, body(): summed = lax.psum(local_sq, 'gx')  35.3 us
    dot_general x2, matrix products, contribute(): jnp.dot(pieces[0], rows_out, preferred_element_type=jnp.float32)  31.8 us
    add x2, other arithmetic, body(): partial_value = keep + from_partner(sent, 'gx', bit)  16 us
    select_n x3, other arithmetic, body(): sent = jnp.where(upper_side, lower, upper)  15.9 us
  transfers between devices with their start and end apart: 5, of which 5 were waited for; matrix products, arithmetic and copies ran while one was open for 11% of the time, Pallas kernels for 0%

commit v1 on v0

--- a/solution.py
+++ b/solution.py
@@ -1,10 +1,284 @@
+import functools
 import jax
 import jax.numpy as jnp
 from jax import lax
+from jax.experimental import pallas as pl
+from jax.experimental.pallas import tpu as pltpu
 from jax.sharding import PartitionSpec as P
 
 D = 16384
 COLB = 8
+ROWS = 128
+SLOTS = 5
+LANES = 256
+IN_FLIGHT = 1
+
+
+def dot32(left, right):
+    return jnp.dot(left, right, preferred_element_type=jnp.float32)
+
+
+def fused_kernel(
+    devices,
+    att_ref, act_ref, res_ref, wo_ref, wd_ref, gain_ref,
+    stream_ref, normed_ref,
+    own_att, own_act, far_att, far_act, res_v, ring_o, ring_d, own_sum,
+    core_out, core_in, chip_out, chip_in, kept, stream_v, normed_v, stat,
+    local_sem, ring_sem, far_send, far_recv, core_send, core_recv, chip_send, chip_recv,
+    stat_send, stat_recv, out_sem,
+):
+    tokens, width_a = own_att.shape
+    width_h = own_act.shape[1]
+    chunks = tokens // ROWS
+    piece = kept.shape[1]
+    total_blocks = COLB * (chunks + 1)
+    me = lax.axis_index("gx")
+    column = lax.rem(me, COLB)
+    group = lax.div(me, COLB)
+    facing = lax.bitwise_xor(me, COLB)
+
+    def ring_copies(n):
+        index = jnp.where(n < COLB, group, 1 - group)
+        slot = lax.rem(n, SLOTS)
+        owner = lax.bitwise_xor(column, COLB - 1 - lax.rem(n, COLB))
+        cols = pl.ds(pl.multiple_of(owner * piece, piece), piece)
+        rows_o = pl.ds(pl.multiple_of(index * width_a, width_a), width_a)
+        rows_d = pl.ds(pl.multiple_of(index * width_h, width_h), width_h)
+        return (
+            pltpu.make_async_copy(wo_ref.at[0, rows_o, cols], ring_o.at[slot], ring_sem.at[0, slot]),
+            pltpu.make_async_copy(wd_ref.at[0, rows_d, cols], ring_d.at[slot], ring_sem.at[1, slot]),
+        )
+
+    def ring_start(n):
+        for copy in ring_copies(n):
+            copy.start()
+
+    def ring_wait(n):
+        for copy in ring_copies(n):
+            copy.wait()
+
+    def far_copies(t):
+        rows = pl.ds(pl.multiple_of(t * ROWS, ROWS), ROWS)
+        return [
+            pltpu.make_async_remote_copy(
+                src_ref=source.at[rows], dst_ref=target.at[rows],
+                send_sem=far_send.at[k, t], recv_sem=far_recv.at[k, t],
+                device_id={"gx": facing}, device_id_type=pl.DeviceIdType.MESH,
+            )
+            for k, (source, target) in enumerate(((att_ref, far_att), (act_ref, far_act)))
+        ]
+
+    def core_copy(t, d):
+        return pltpu.make_async_remote_copy(
+            src_ref=core_out.at[d], dst_ref=core_in.at[t, d],
+            send_sem=core_send.at[d], recv_sem=core_recv.at[t, d],
+            device_id={"gx": lax.bitwise_xor(me, 1)}, device_id_type=pl.DeviceIdType.MESH,
+        )
+
+    def chip_copy(t, d):
+        return pltpu.make_async_remote_copy(
+            src_ref=chip_out.at[d], dst_ref=chip_in.at[t, d],
+            send_sem=chip_send.at[d], recv_sem=chip_recv.at[t, d],
+            device_id={"gx": lax.bitwise_xor(me, COLB - 2 - 2 * d)}, device_id_type=pl.DeviceIdType.MESH,
+        )
+
+    def stat_copy(distance):
+        peer = lax.bitwise_xor(me, distance)
+        return pltpu.make_async_remote_copy(
+            src_ref=stat.at[0], dst_ref=stat.at[distance],
+            send_sem=stat_send.at[distance], recv_sem=stat_recv.at[distance],
+            device_id={"gx": peer}, device_id_type=pl.DeviceIdType.MESH,
+        )
+
+    own_copies = [
+        pltpu.make_async_copy(att_ref, own_att, local_sem.at[0]),
+        pltpu.make_async_copy(act_ref, own_act, local_sem.at[1]),
+        pltpu.make_async_copy(res_ref, res_v, local_sem.at[2]),
+    ]
+    barrier = pltpu.get_barrier_semaphore()
+
+    @pl.loop(1, devices)
+    def _(distance):
+        pl.semaphore_signal(
+            barrier, inc=1, device_id={"gx": lax.bitwise_xor(me, distance)},
+            device_id_type=pl.DeviceIdType.MESH,
+        )
+
+    for copy in own_copies:
+        copy.start()
+    for n in range(SLOTS):
+        ring_start(n)
+    pl.semaphore_wait(barrier, devices - 1)
+    for t in range(IN_FLIGHT):
+        for copy in far_copies(t):
+            copy.start()
+    for copy in own_copies:
+        copy.wait()
+
+    def refill(n):
+        @pl.when(n + SLOTS < total_blocks)
+        def _():
+            ring_start(n + SLOTS)
+
+    @pl.loop(0, COLB)
+    def _(j):
+        ring_wait(j)
+        slot = lax.rem(j, SLOTS)
+
+        @pl.loop(0, piece // LANES)
+        def _(i):
+            cols = pl.ds(pl.multiple_of(i * LANES, LANES), LANES)
+            own_sum[j, :, cols] = dot32(own_att[...], ring_o[slot, :, cols]) + dot32(
+                own_act[...], ring_d[slot, :, cols]
+            )
+
+        refill(j)
+
+    @pl.loop(0, chunks)
+    def _(t):
+        rows = pl.ds(pl.multiple_of(t * ROWS, ROWS), ROWS)
+        for copy in far_copies(t):
+            copy.wait()
+
+        @pl.when(t + IN_FLIGHT < chunks)
+        def _():
+            for copy in far_copies(t + IN_FLIGHT):
+                copy.start()
+
+        def multiply(j, write):
+            n = COLB * (t + 1) + j
+            ring_wait(n)
+            slot = lax.rem(n, SLOTS)
+
+            @pl.loop(0, piece // LANES)
+            def _(i):
+                cols = pl.ds(pl.multiple_of(i * LANES, LANES), LANES)
+                write(
+                    cols,
+                    own_sum[j, rows, cols]
+                    + dot32(far_att[rows, :], ring_o[slot, :, cols])
+                    + dot32(far_act[rows, :], ring_d[slot, :, cols]),
+                )
+
+            refill(n)
+
+        @pl.loop(0, COLB // 2)
+        def _(d):
+            def to_core(cols, value):
+                core_out[d, :, cols] = value.astype(jnp.bfloat16)
+
+            multiply(2 * d, to_core)
+            core_copy(t, d).start()
+
+            def keep(cols, value):
+                kept[:, cols] = value
+
+            multiply(2 * d + 1, keep)
+            core_copy(t, d).wait_recv()
+
+            @pl.when(d < COLB // 2 - 1)
+            def _():
+                chip_out[d] = (kept[...] + core_in[t, d].astype(jnp.float32)).astype(jnp.bfloat16)
+                chip_copy(t, d).start()
+
+        last = COLB // 2 - 1
+        total = kept[...] + core_in[t, last].astype(jnp.float32) + res_v[rows].astype(jnp.float32)
+        for d in range(last):
+            chip_copy(t, d).wait_recv()
+            total = total + chip_in[t, d].astype(jnp.float32)
+        stream = total.astype(jnp.bfloat16)
+        stream_v[rows] = stream
+        wide = stream.astype(jnp.float32)
+        square = wide * wide
+        folded = square[:, :128]
+        for k in range(1, piece // 128):
+            folded = folded + square[:, k * 128:(k + 1) * 128]
+        stat[0, t] = jnp.sum(jnp.transpose(folded), axis=0, keepdims=True)
+        for d in range(last + 1):
+            core_copy(t, d).wait_send()
+        for d in range(last):
+            chip_copy(t, d).wait_send()
+
+    stream_out = pltpu.make_async_copy(stream_v, stream_ref, out_sem.at[0])
+    stream_out.start()
+
+    @pl.loop(1, devices)
+    def _(distance):
+        stat_copy(distance).start()
+
+    @pl.loop(1, devices)
+    def _(distance):
+        stat_copy(distance).wait()
+
+    summed = jnp.sum(stat[...], axis=0)
+    scale = lax.rsqrt(summed / D + 1e-05)
+    for t in range(chunks):
+        factor = jnp.transpose(jnp.broadcast_to(scale[t], (128, ROWS)))
+        for k in range(piece // 128):
+            lanes = slice(k * 128, (k + 1) * 128)
+            wide = stream_v[t * ROWS:(t + 1) * ROWS, lanes].astype(jnp.float32)
+            value = wide * factor * gain_ref[:, lanes].astype(jnp.float32)
+            normed_v[t * ROWS:(t + 1) * ROWS, lanes] = value.astype(jnp.bfloat16)
+    normed_out = pltpu.make_async_copy(normed_v, normed_ref, out_sem.at[1])
+    normed_out.start()
+    normed_out.wait()
+    stream_out.wait()
+
+
+def fused(attention, activated, residual, out_tiles, down_tiles, norm_gain):
+    tokens, width_a = attention.shape
+    width_h = activated.shape[1]
+    piece = residual.shape[1]
+    devices = lax.axis_size("gx")
+    chunks = tokens // ROWS
+    half = COLB // 2
+    bf16, f32 = jnp.bfloat16, jnp.float32
+    anywhere = pl.BlockSpec(memory_space=pl.ANY)
+    dma = pltpu.SemaphoreType.DMA
+    shape = jax.ShapeDtypeStruct((tokens, piece), bf16)
+    return pl.pallas_call(
+        functools.partial(fused_kernel, devices),
+        out_shape=(shape, shape),
+        in_specs=[anywhere] * 5 + [pl.BlockSpec(memory_space=pltpu.VMEM)],
+        out_specs=(anywhere, anywhere),
+        scratch_shapes=[
+            pltpu.VMEM((tokens, width_a), bf16),
+            pltpu.VMEM((tokens, width_h), bf16),
+            pltpu.VMEM((tokens, width_a), bf16),
+            pltpu.VMEM((tokens, width_h), bf16),
+            pltpu.VMEM((tokens, piece), bf16),
+            pltpu.VMEM((SLOTS, width_a, piece), bf16),
+            pltpu.VMEM((SLOTS, width_h, piece), bf16),
+            pltpu.VMEM((COLB, tokens, piece), f32),
+            pltpu.VMEM((half, ROWS, piece), bf16),
+            pltpu.VMEM((chunks, half, ROWS, piece), bf16),
+            pltpu.VMEM((half - 1, ROWS, piece), bf16),
+            pltpu.VMEM((chunks, half - 1, ROWS, piece), bf16),
+            pltpu.VMEM((ROWS, piece), f32),
+            pltpu.VMEM((tokens, piece), bf16),
+            pltpu.VMEM((tokens, piece), bf16),
+            pltpu.VMEM((devices, chunks, 1, ROWS), f32),
+            dma((3,)),
+            dma((2, SLOTS)),
+            dma((2, chunks)),
+            dma((2, chunks)),
+            dma((half,)),
+            dma((chunks, half)),
+            dma((half - 1,)),
+            dma((chunks, half - 1)),
+            dma((devices,)),
+            dma((devices,)),
+            dma((2,)),
+        ],
+        compiler_params=pltpu.CompilerParams(
+            collective_id=0, has_side_effects=True, vmem_limit_bytes=63 * 1024 * 1024
+        ),
+        cost_estimate=pl.CostEstimate(
+            flops=2 * tokens * 2 * (width_a + width_h) * COLB * piece,
+            bytes_accessed=2 * (width_a + width_h) * COLB * piece * (chunks + 1),
+            transcendentals=0,
+        ),
+    )(attention, activated, residual, out_tiles, down_tiles, norm_gain.reshape(1, piece))
 
 
 def shifted(block, axis, distance):
@@ -79,8 +353,9 @@
         P("gx", None, None),
         P("gx"),
     )
+    two_groups = mesh.shape["gx"] == 2 * COLB
     return jax.shard_map(
-        body,
+        fused if two_groups else body,
         mesh=mesh,
         in_specs=placed,
         out_specs=(P("groups", "gx"), P("groups", "gx")),

time: 513 us -> 163 us (0.32)
  waiting for transfers between devices: 337 us -> 0 us
  Pallas kernels: 0 us -> 157 us
  matrix products: 89.2 us -> 0 us
  other arithmetic: 36 us -> 0 us
  blocking collectives: 35.3 us -> 0 us
  starting transfers between devices: 6.34 us -> 0 us
    ppermute x5 -> x0, waiting for transfers between devices: 337 us -> none  [the longest x3 275 us: from_partner(): lax.ppermute(array, axis, [(i, i ^ 1 << stride) for i in range(lax.axis_s...]
    pallas_call x0 -> x1, Pallas kernels: none -> 157 us  [fused(): pl.pallas_call(functools.partial(fused_kernel, devices), out_shape=(shape...]
    dot_general x4 -> x0, matrix products: 89.2 us -> none  [the longest x2 57.3 us: contribute(): jnp.dot(pieces[1], rows_down, preferred_element_type=jnp.float32)]
    psum x1 -> x0, blocking collectives: 35.3 us -> none  [body(): summed = lax.psum(local_sq, 'gx')]
    add x2 -> x0, other arithmetic: 16 us -> none  [body(): partial_value = keep + from_partner(sent, 'gx', bit)]
    select_n x3 -> x0, other arithmetic: 15.9 us -> none  [body(): sent = jnp.where(upper_side, lower, upper)]
    ppermute x5 -> x0, starting transfers between devices: 6.34 us -> none  [the longest x2 4.18 us: shifted(): return lax.ppermute(block, axis, route)]
  transfers between devices with their start and end apart: 5 -> 0, of which waited for: 5 -> 0; matrix products, arithmetic and copies ran while one was open for 11% -> 0% of each run, Pallas kernels for 0% -> 0%
where the time goes in v1:
time: 163 us
  Pallas kernels  157 us (96%)
  local copies, waits for them, and re-layouts  5.8 us (4%)
    pallas_call x1, Pallas kernels, fused(): pl.pallas_call(functools.partial(fused_kernel, devices), out_shape=(shape...  157 us
    unnamed x2, local copies, waits for them, and re-layouts  4.52 us

profile of v1, /device:TPU:0, one launch (start us, length us, event | category | flops | bytes accessed | tf_op | source)
XLA Modules:
  0.0 163.0 jit_solution(9032355319112408213)
XLA Ops:
  0.6 1.3 reshape.7.gain_ref
  1.9 156.6 %shard_map.77 = (bf16[512,1024]{1,0:T(8,128)(2,1)}, bf16[512,1024]{1,0:T(8,128)(2,1)}) custom-call(bf16[512,1024]{1,0:T(8,128)(2,1)} %att_ref.1, bf16[512,1664]{1,0:T(8,128)(2,1)} %act_ref.1, bf16[512,1024]{1,0:T(8,128)(2,1)} %res_ref.1, bf16[1,2048,8192]{2,1,0:T(8,128)(2,1)} %wo_ref.1, bf16[1,3328,8192]{2,1,0:T(8,128)(2,1)} %wd_ref.1, ...), custom_call_target="tpu_custom_call" | custom-call | flops 45097156608 | bytes 220200960 | tf_op jit(solution)/shard_map/pallas_call | solution.py:239
  158.5 2.3 %copy.10 = bf16[512,1024]{1,0:T(8,128)(2,1)} copy(bf16[512,1024]{1,0:T(8,128)(2,1)} %get-tuple-element.4) | data formatting | bytes 2097152
  160.8 2.3 %copy.11 = bf16[512,1024]{1,0:T(8,128)(2,1)} copy(bf16[512,1024]{1,0:T(8,128)(2,1)} %get-tuple-element.5) | data formatting | bytes 2097152
